TPU v7x, 32 devices: a whole 2x2x4 slice. The times are simulated.
32 devices in a mesh: tm: 4 (over z), docs: 8 (over y, x, core).
Axes of the slice: x: 2, y: 2, z: 4, core: 2. Of those that a mesh axis runs over, the one named last changes fastest.
Arguments:
- counts: int32 [4, 512, 32768], P('tm', 'docs'), may hold values from 0 to 5, as said below
- topic_means: float32 [4, 32768, 128], P('tm', 'docs'), may hold values from -80 to 170
- doc_topics_init: float32 [4, 512, 128], P('tm', 'docs'), may hold values from 0.5 to 20
- dirichlet_prior: float32 [128], replicated, may hold values from 0.05 to 1
- chain_var: float32 [128], replicated, may hold values from 0.005 to 0.5
- obs_noise: float32 [128], replicated, may hold values from 0.1 to 10
Outputs:
- smoothed_means: float32 [4, 32768, 128], P('tm', 'docs')
- doc_topics: float32 [4, 512, 128], P('tm', 'docs')
Inputs may be any that keep to these rules, and one draw needn't show every extreme that they name: `counts`: each entry is 0 or a count of 1 to 5; each word has its own share of nonzero entries, between a quarter and three quarters.
All inputs are finite; a program needn't handle non-finite values.
Results may differ from a plain program's by a relative error of at most 0.01.
Values may be sent and summed in bfloat16 or wider, within the bound.
A program may use at most 128 MiB of HBM per device.

v0:
```python
import jax
import jax.numpy as jnp
from jax import lax
from jax.sharding import PartitionSpec as P

V = 32768
ITERS_E = 4


prior_count = 0.5
initial_scale = 1000.0


def as_sent(shard):

    def short(part):
        return part.astype(jnp.bfloat16) if part.dtype == jnp.float32 else part

    return jax.tree.map(short, shard)


def chain_factors(totals, chain_var, obs_noise):
    relative = jnp.sum(totals, axis=1, keepdims=True) / (totals.shape[1] * totals)
    noise = obs_noise[None, :] * relative

    def advance(previous, noise_level):
        predicted = previous + chain_var
        own_gain = predicted / (predicted + noise_level)
        current = (1.0 - own_gain) * predicted
        return (current, (own_gain, current))

    unused, (gains, filtered_var) = lax.scan(advance, initial_scale * chain_var, noise)
    smooth = filtered_var / (filtered_var + chain_var)
    smooth = jnp.concatenate([smooth[:-1], jnp.zeros_like(smooth[-1:])], axis=0)
    return (gains, smooth)


def body(counts, topic_means, doc_topics_init, dirichlet_prior, chain_var, obs_noise):
    topic_slab = topic_means[0]
    concentration = doc_topics_init[0]
    count_wide = counts[0].astype(jnp.float32)
    local_peak = jnp.max(topic_slab, axis=0)
    column_peak = lax.pmax(local_peak, "docs")
    column_mass = lax.psum(jnp.sum(jnp.exp(topic_slab - column_peak[None, :]), axis=0), "docs")
    beta_slab = jnp.exp(topic_slab - (column_peak + jnp.log(column_mass))[None, :]).astype(
        jnp.bfloat16
    )
    beta_full = lax.all_gather(beta_slab, "docs", axis=0, tiled=True)
    for sweep_index in range(ITERS_E):
        proportions = jnp.exp(lax.digamma(concentration)).astype(jnp.bfloat16)
        mixture = lax.dot_general(
            proportions, beta_full, (((1,), (1,)), ((), ())), preferred_element_type=jnp.float32
        )
        ratios = (count_wide / mixture).astype(jnp.bfloat16)
        update = proportions.astype(jnp.float32) * jnp.dot(
            ratios, beta_full, preferred_element_type=jnp.float32
        )
        concentration = dirichlet_prior[None, :] + update
    word_stats = lax.psum_scatter(
        (
            beta_full.astype(jnp.float32)
            * lax.dot_general(
                ratios, proportions, (((0,), (0,)), ((), ())), preferred_element_type=jnp.float32
            )
        ).astype(jnp.bfloat16),
        "docs",
        scatter_dimension=0,
        tiled=True,
    ).astype(jnp.float32)
    slice_index = lax.axis_index("tm")
    slices = lax.axis_size("tm")
    own_row = (jnp.arange(slices) == slice_index).astype(jnp.float32)
    placed = own_row[:, None] * jnp.sum(update, axis=0)[None, :]
    totals = lax.psum(placed, ("tm", "docs"))
    gains, smooth = chain_factors(totals, chain_var, obs_noise)
    own_total = jnp.sum(own_row[:, None] * totals, axis=0)
    own_gain = jnp.sum(own_row[:, None] * gains, axis=0)
    own_factor = jnp.sum(own_row[:, None] * smooth, axis=0)
    pseudo = jnp.log(word_stats + prior_count) - jnp.log((own_total + prior_count * V) / V)[None, :]
    forward_rate = 1.0 - own_gain
    forward_term = own_gain[None, :] * pseudo
    forward_logs = jnp.cumsum(jnp.log(1.0 - gains), axis=0)
    prior_row = (jnp.arange(slices) == slice_index - 1).astype(jnp.float32)
    reach_forward = jnp.sum(prior_row[:, None] * forward_logs, axis=0)
    shard_piece = lax.all_gather(
        forward_term[None].astype(jnp.bfloat16), "tm", axis=0, tiled=True
    ).astype(jnp.float32)
    sources = jnp.arange(shard_piece.shape[0])
    log_rows = forward_logs
    earlier_mask = (sources < slice_index)[:, None]
    weight = jnp.where(
        earlier_mask, jnp.exp(jnp.minimum(reach_forward[None, :] - log_rows, 0.0)), 0.0
    )
    entering = jnp.zeros_like(forward_term) + jnp.einsum("rk,rwk->wk", weight, shard_piece)
    filtered = forward_rate[None, :] * entering + forward_term
    back_term = (1.0 - own_factor)[None, :] * filtered
    last_row = (jnp.arange(slices) == slices - 1)[:, None]
    backward_logs = jnp.cumsum(jnp.log(jnp.where(last_row, 1.0, smooth)), axis=0)
    shifted_logs = jnp.concatenate([jnp.zeros_like(backward_logs[:1]), backward_logs[:-1]], axis=0)
    reach_back = jnp.sum(own_row[:, None] * backward_logs, axis=0)
    shard_piece = lax.all_gather(as_sent(back_term[None]), "tm", axis=0, tiled=True)
    sources = jnp.arange(shard_piece.shape[0])
    log_rows = shifted_logs
    later_mask = (sources > slice_index)[:, None]
    weight = jnp.where(later_mask, jnp.exp(jnp.minimum(log_rows - reach_back[None, :], 0.0)), 0.0)
    following = jnp.zeros_like(back_term) + jnp.einsum("rk,rwk->wk", weight, shard_piece)
    smoothed = own_factor[None, :] * following + back_term
    return (smoothed[None], concentration[None])


def solution(mesh):
    in_specs = (P("tm", "docs", None), P("tm", "docs", None), P("tm", "docs", None), P(), P(), P())
    out_specs = (P("tm", "docs", None), P("tm", "docs", None))
    return jax.shard_map(body, mesh=mesh, in_specs=in_specs, out_specs=out_specs, check_vma=False)
```

profile of v0, /device:TPU:0, one launch (start us, length us, event | category | flops | bytes accessed | tf_op | source)
XLA Modules:
  0.0 402.4 jit_solution(17428700434300192266)
XLA Ops:
  7.2 0.0 copy-start.1
  7.2 0.0 copy-start.4
  7.2 0.0 copy-start.7
  7.2 0.0 all-gather.6.cloned.1.call-start
  7.2 2.3 reduce_max.9
  9.5 15.1 %pmax.7 = f32[128]{0:T(128)S(1)} all-reduce(f32[128]{0:T(128)S(1)} %reduce_max.9), channel_id=1, replica_groups=mesh['tm'=4,'docs'=8] {'docs'}, use_global_device_ids=true, to_apply=%region_1.0 | all-reduce | flops 128 | bytes 1024 | tf_op jit(solution)/shard_map/pmax | solution.py:43
  24.6 2.2 fusion.8
  26.8 11.8 %psum.14 = f32[128]{0:T(128)S(1)} all-reduce(f32[128]{0:T(128)S(1)} %fusion.8), channel_id=1, replica_groups=mesh['tm'=4,'docs'=8] {'docs'}, use_global_device_ids=true, to_apply=%region_3.0 | all-reduce | flops 128 | bytes 1024 | tf_op jit(solution)/shard_map/psum | solution.py:44
  38.6 0.0 copy-done.1
  38.6 1.3 fusion.10
  39.8 0.0 all-gather.6.cloned.1.call-update
  39.9 0.0 reduce-scatter.2.cloned.1.call-start
  39.9 53.9 %all-gather.6.cloned.1.call-done = bf16[32768,128]{1,0:T(8,128)(2,1)} async-done(((bf16[4096,128]{1,0:T(8,128)(2,1)}), bf16[32768,128]{1,0:T(8,128)(2,1)}) %all-gather.6.cloned.1.call-update) | async-done | bytes 8388624 | tf_op jit(solution)/shard_map/all_gather | solution.py:48
  93.8 0.0 copy-done.4
  93.8 0.0 copy-done.7
  93.8 13.1 %fusion.29 = bf16[64,128]{1,0:T(8,128)(2,1)S(1)} fusion(bf16[32768,128]{1,0:T(8,128)(2,1)} %all-gather.6.cloned.1.call-done, s32[1,64,32768]{2,1,0:T(8,128)} %param.8, f32[1,64,128]{2,1,0:T(8,128)S(1)} %copy-done.7, f32[128]{0:T(128)S(1)} %copy-done.4), kind=kOutput, calls=%fused_computation.52 | convolution fusion | flops 1081925632 | bytes 16826880 | tf_op jit(solution)/shard_map/dot_general | solution.py:55
  106.9 12.6 %fusion.33 = bf16[64,128]{1,0:T(8,128)(2,1)S(1)} fusion(bf16[32768,128]{1,0:T(8,128)(2,1)} %all-gather.6.cloned.1.call-done, bf16[64,128]{1,0:T(8,128)(2,1)S(1)} %fusion.29, s32[1,64,32768]{2,1,0:T(8,128)} %param.8, f32[128]{0:T(128)S(1)} %copy-done.4), kind=kOutput, calls=%fused_computation.56 | convolution fusion | flops 1080680448 | bytes 16810496 | tf_op jit(solution)/shard_map/dot_general | solution.py:55
  119.4 12.3 %fusion.16 = f32[64,128]{1,0:T(8,128)S(1)} fusion(bf16[32768,128]{1,0:T(8,128)(2,1)} %all-gather.6.cloned.1.call-done, bf16[64,128]{1,0:T(8,128)(2,1)S(1)} %fusion.33, s32[1,64,32768]{2,1,0:T(8,128)} %param.8, f32[128]{0:T(128)S(1)} %copy-done.4), kind=kOutput, calls=%fused_computation.31 | convolution fusion | flops 1080057856 | bytes 16826880 | tf_op jit(solution)/shard_map/dot_general | solution.py:55
  131.8 9.2 %fusion.1 = bf16[64,32768]{1,0:T(8,128)(2,1)S(1)} fusion(bf16[32768,128]{1,0:T(8,128)(2,1)} %all-gather.6.cloned.1.call-done, s32[1,64,32768]{2,1,0:T(8,128)} %param.8, f32[64,128]{1,0:T(8,128)S(1)} %fusion.16), kind=kOutput, calls=%fused_computation.5 | convolution fusion | flops 543784960 | bytes 21004288 | tf_op jit(solution)/shard_map/dot_general | solution.py:51
  141.0 0.0 copy-start
  141.0 1.9 copy-done
  142.9 7.3 %fusion = bf16[32768,128]{1,0:T(8,128)(2,1)} fusion(bf16[64,32768]{1,0:T(8,128)(2,1)S(1)} %fusion.1, bf16[32768,128]{1,0:T(8,128)(2,1)} %all-gather.6.cloned.1.call-done, f32[64,128]{1,0:T(8,128)S(1)} %fusion.16), kind=kOutput, calls=%fused_computation.3 | convolution fusion | flops 550076416 | bytes 21004288 | tf_op jit(solution)/shard_map/dot_general | solution.py:62
  150.2 0.0 reduce-scatter.2.cloned.1.call-update
  150.2 0.0 all-gather.8.cloned.1.call-start
  150.3 0.5 copy-done.3
  150.9 7.0 %add_bitcast_fusion = (f32[1,64,128]{2,1,0:T(8,128)}, f32[128]{0:T(128)S(1)}) fusion(f32[128]{0:T(128)S(1)} %copy-done.4, bf16[64,32768]{1,0:T(8,128)(2,1)} %copy-done, bf16[32768,128]{1,0:T(8,128)(2,1)} %all-gather.6.cloned.1.call-done, f32[64,128]{1,0:T(8,128)S(1)} %fusion.16), kind=kOutput, calls=%fused_computation.72 | convolution fusion | flops 537526144 | bytes 12649472 | tf_op jit(solution)/shard_map/dot_general | solution.py:55
  157.9 0.1 broadcast_multiply_fusion
  158.0 39.6 %psum.15 = f32[4,128]{1,0:T(4,128)S(1)} all-reduce(f32[4,128]{1,0:T(4,128)S(1)} %broadcast_multiply_fusion), channel_id=1, replica_groups=mesh['tm'=4,'docs'=8] {'tm','docs'}, use_global_device_ids=true, to_apply=%region_5.0 | all-reduce | flops 512 | bytes 4096 | tf_op jit(solution)/shard_map/psum | solution.py:74
  197.6 0.1 fusion.258
  197.7 0.0 copy-done.5
  197.7 0.1 divide_multiply_fusion
  197.8 0.4 while.15
  198.2 0.1 select_log_fusion
  198.3 0.1 multiply_reduce_fusion.2
  198.4 24.0 %reduce-scatter.2.cloned.1.call-done = bf16[4096,128]{1,0:T(8,128)(2,1)} async-done(((bf16[32768,128]{1,0:T(8,128)(2,1)}), bf16[4096,128]{1,0:T(8,128)(2,1)}) %reduce-scatter.2.cloned.1.call-update) | async-done | bytes 1048592 | tf_op jit(solution)/shard_map/reduce_scatter | solution.py:59
  222.4 2.7 fusion.11
  225.1 0.0 all-gather.8.cloned.1.call-update
  225.1 0.0 all-gather.10.cloned.1.call-start
  225.2 0.1 multiply_reduce_fusion.3
  225.3 0.1 select_bitcast_fusion.1
  225.4 80.6 %all-gather.8.cloned.1.call-done = bf16[16384,128]{1,0:T(8,128)(2,1)} async-done(((bf16[4096,128]{1,0:T(8,128)(2,1)}), bf16[16384,128]{1,0:T(8,128)(2,1)}) %all-gather.8.cloned.1.call-update) | async-done | bytes 4194320 | tf_op jit(solution)/shard_map/all_gather | solution.py:85
  306.0 3.3 multiply_reduce_fusion.1
  309.3 1.7 fusion.21
  310.9 0.0 all-gather.10.cloned.1.call-update
  311.0 0.1 select_bitcast_fusion
  311.0 79.4 %all-gather.10.cloned.1.call-done = bf16[16384,128]{1,0:T(8,128)(2,1)} async-done(((bf16[4096,128]{1,0:T(8,128)(2,1)}), bf16[16384,128]{1,0:T(8,128)(2,1)}) %all-gather.10.cloned.1.call-update) | async-done | bytes 4194320 | tf_op jit(solution)/shard_map/all_gather | solution.py:101
  390.4 3.3 multiply_reduce_fusion
  393.7 2.1 fusion.5
  (31 shorter events, 0.5 us)
Async XLA Ops:
  7.2 31.4 %copy-start.1 = (f32[1,4096,128]{2,1,0:T(8,128)S(1)}, f32[1,4096,128]{2,1,0:T(8,128)}, u32[]{:S(2)}) copy-start(f32[1,4096,128]{2,1,0:T(8,128)} %param.9) | copy-start | bytes 6291460
  7.2 86.6 %copy-start.4 = (f32[128]{0:T(128)S(1)}, f32[128]{0:T(128)}, u32[]{:S(2)}) copy-start(f32[128]{0:T(128)} %param.11) | copy-start | bytes 1540
  7.2 86.6 %copy-start.7 = (f32[1,64,128]{2,1,0:T(8,128)S(1)}, f32[1,64,128]{2,1,0:T(8,128)}, u32[]{:S(2)}) copy-start(f32[1,64,128]{2,1,0:T(8,128)} %param.10) | copy-start | bytes 98308
  7.2 86.6 %all-gather.6.cloned.1.call-start = ((), (), s32[]{:S(2)}) async-start(), calls=%async_computation.1 | async-start | bytes 9437184 | tf_op jit(solution)/shard_map/all_gather | solution.py:48
  39.9 182.5 %reduce-scatter.2.cloned.1.call-start = ((), (), s32[]{:S(2)}) async-start(), calls=%async_computation.2 | async-start | bytes 9437184 | tf_op jit(solution)/shard_map/reduce_scatter | solution.py:59
  141.0 1.9 copy-start
  150.2 0.7 copy-start.3
  150.2 155.7 %all-gather.8.cloned.1.call-start = ((), (), s32[]{:S(2)}) async-start(), calls=%async_computation.3 | async-start | bytes 5242880 | tf_op jit(solution)/shard_map/all_gather | solution.py:85
  150.9 46.8 %copy-start.5 = (f32[128]{0:T(128)S(1)}, f32[128]{0:T(128)}, u32[]{:S(2)}) copy-start(f32[128]{0:T(128)} %param.13) | copy-start | bytes 1540
  150.9 47.3 %copy-start.6 = (pred[4]{0:T(512)(128)(4,1)S(1)}, pred[4]{0:T(512)(128)(4,1)}, u32[]{:S(2)}) copy-start(pred[4]{0:T(512)(128)(4,1)} %constant.19.clone.1) | copy-start | bytes 16
  225.1 84.2 %copy-start.2 = (bf16[4096,128]{1,0:T(8,128)(2,1)S(1)}, bf16[4096,128]{1,0:T(8,128)(2,1)}, u32[]{:S(2)}) copy-start(bf16[4096,128]{1,0:T(8,128)(2,1)} %reduce-scatter.2.cloned.1.call-done) | copy-start | bytes 3145732
  225.1 165.3 %all-gather.10.cloned.1.call-start = ((), (), s32[]{:S(2)}) async-start(), calls=%async_computation.4 | async-start | bytes 5242880 | tf_op jit(solution)/shard_map/all_gather | solution.py:101
Sparse Core Ops, SparseCore 0:
  40.0 53.7 all-gather.5
  150.4 71.9 reduce-scatter.1
  225.2 80.7 all-gather.7
  311.1 79.2 all-gather.9
where the time goes:
time: 403 us; the launch traced here: 402 us
  waiting for transfers between devices  238 us (59%)
  blocking collectives  66.5 us (17%)
  matrix products  61.5 us (15%)
  other arithmetic  19.6 us (5%)
  between operations  13.9 us (3%)
    all_gather x1, waiting for transfers between devices, body(): lax.all_gather(forward_term[None].astype(jnp.bfloat16), 'tm', axis=0, til...  80.6 us
    all_gather x1, waiting for transfers between devices, body(): lax.all_gather(as_sent(back_term[None]), 'tm', axis=0, tiled=True)  79.4 us
    all_gather x1, waiting for transfers between devices, body(): beta_full = lax.all_gather(beta_slab, 'docs', axis=0, tiled=True)  53.9 us
    dot_general x4, matrix products, body(): jnp.dot(ratios, beta_full, preferred_element_type=jnp.float32)  45 us
    psum x1, blocking collectives, body(): totals = lax.psum(placed, ('tm', 'docs'))  39.6 us
    reduce_scatter x1, waiting for transfers between devices, body(): lax.psum_scatter((beta_full.astype(jnp.float32) * lax.dot_general(ratios,...  24 us
    pmax x1, blocking collectives, body(): column_peak = lax.pmax(local_peak, 'docs')  15.1 us
    psum x1, blocking collectives, body(): lax.psum(jnp.sum(jnp.exp(topic_slab - column_peak[None, :]), axis=0), 'do...  11.8 us
  transfers between devices with their start and end apart: 4, of which 4 were waited for; matrix products, arithmetic and copies ran while one was open for 2% of the time, Pallas kernels for 0%

commit v1 on v0

v1 whole, which is shorter than its diff:
```python
import functools

import jax
import jax.numpy as jnp
from jax import lax
from jax.experimental import pallas as pl
from jax.experimental.pallas import tpu as pltpu
from jax.sharding import PartitionSpec as P

ITERS_E = 4
prior_count = 0.5
initial_scale = 1000.0
MESH = pl.DeviceIdType.MESH
BF = jnp.bfloat16
F32 = jnp.float32


def expected_proportions(x):
    u = x * (x + 5.0)
    steps = (2.0 * x + 5.0) * (1.0 / u + 1.0 / (u + 4.0) + 1.0 / (u + 6.0))
    y = x + 6.0
    inv = 1.0 / y
    sq = inv * inv
    tail = sq * (1.0 / 12 - sq * (1.0 / 120 - sq * (1.0 / 252 - sq * (1.0 / 240))))
    return jnp.exp(jnp.log(y) - 0.5 * inv - tail - steps)


def round_kernel(n, slices, word_tile, chunk, counts_ref, slab_ref, init_ref, prior_ref, chain_ref,
                 obs_ref, smooth_ref, topics_ref, raw, outgoing, ratio, weights, beta, theta,
                 acc, part_out, part_in, stat_out, stat_in, tot_out, tot_in, row_out, row_in,
                 fwd_in, back_in, fwd_out, back_out, load_sem, cnt_s, cnt_r, theta_s, theta_r,
                 part_s, part_r, stat_s, stat_r, tot_s, tot_r, row_s, row_r, fwd_s, fwd_r,
                 back_s, back_r):
    docs = init_ref.shape[0]
    words = slab_ref.shape[0]
    me = lax.axis_index("docs")
    now = lax.axis_index("tm")

    def peers(fn, size, own):
        def step(m, carry):
            fn(lax.rem(own + m, size))
            return carry
        lax.fori_loop(1, size, step, 0)

    def rows(p):
        return pl.ds(pl.multiple_of(p * docs, docs), docs)

    def load(p):
        return pltpu.make_async_copy(
            counts_ref.at[:, pl.ds(pl.multiple_of(p * words, words), words)], raw.at[p],
            load_sem.at[p])

    def to_docs(src, dst, s, r, p):
        return pltpu.make_async_remote_copy(src_ref=src, dst_ref=dst, send_sem=s, recv_sem=r,
                                            device_id={"docs": p}, device_id_type=MESH)

    def to_tm(src, dst, s, r, p):
        return pltpu.make_async_remote_copy(src_ref=src, dst_ref=dst, send_sem=s, recv_sem=r,
                                            device_id={"tm": p}, device_id_type=MESH)

    def load_all(p, carry):
        load(p).start()
        return carry

    lax.fori_loop(0, n, load_all, 0)

    barrier = pltpu.get_barrier_semaphore()
    peers(lambda p: pl.semaphore_signal(barrier, inc=1, device_id={"docs": p},
                                        device_id_type=MESH), n, me)
    peers(lambda p: pl.semaphore_signal(barrier, inc=1, device_id={"tm": p},
                                        device_id_type=MESH), slices, now)

    first = expected_proportions(init_ref[...]).astype(BF)
    theta[0, rows(me), :] = first
    peak = jnp.max(slab_ref[...], axis=0, keepdims=True)
    weights[...] = jnp.exp(slab_ref[...] - peak)
    mass = jnp.sum(weights[...], axis=0, keepdims=True)
    eight = (8, peak.shape[1])
    stat_out[0] = jnp.broadcast_to(peak, eight)
    stat_out[1] = jnp.broadcast_to(mass, eight)
    pl.semaphore_wait(barrier, n - 1 + slices - 1)

    def theta_copy(it, src_block, p, r):
        block = theta.at[it, rows(src_block), :]
        return to_docs(block, block, theta_s.at[it, p], theta_r.at[it, r], p)

    def stat_copy(src_block, p):
        return to_docs(stat_out, stat_in.at[src_block], stat_s.at[p], stat_r.at[src_block], p)

    def cnt_copy(src_block, p):
        return to_docs(outgoing.at[p], ratio.at[rows(src_block), :], cnt_s.at[p],
                       cnt_r.at[src_block], p)

    def part_copy(it, src_block, p):
        return to_docs(part_out.at[it, rows(p), :], part_in.at[it, src_block],
                       part_s.at[it, p], part_r.at[it, src_block], p)

    def tot_copy(src_block, p):
        return to_docs(tot_out, tot_in.at[src_block], tot_s.at[p], tot_r.at[src_block], p)

    def row_copy(src_block, p):
        return to_tm(row_out, row_in.at[src_block], row_s.at[p], row_r.at[src_block], p)

    peers(lambda p: stat_copy(me, p).start(), n, me)
    peers(lambda p: theta_copy(0, me, p, me).start(), n, me)

    def send_counts(p):
        load(p).wait()
        outgoing[p] = raw[p].astype(F32).astype(BF)
        cnt_copy(me, p).start()

    peers(send_counts, n, me)
    load(me).wait()
    ratio[rows(me), :] = raw[me].astype(F32).astype(BF)

    stat_in[me] = stat_out[...]
    peers(lambda q: stat_copy(q, q).wait_recv(), n, me)
    all_peaks = [stat_in[q, 0, 0:1, :] for q in range(n)]
    top = functools.reduce(jnp.maximum, all_peaks)
    total_mass = sum(stat_in[q, 1, 0:1, :] * jnp.exp(all_peaks[q] - top) for q in range(n))
    beta[...] = (weights[...] * (jnp.exp(peak - top) / total_mass)).astype(BF)

    peers(lambda q: theta_copy(0, q, q, q).wait_recv(), n, me)
    peers(lambda q: cnt_copy(q, q).wait_recv(), n, me)

    prior = prior_ref[...]
    for it in range(ITERS_E):
        last = it == ITERS_E - 1
        acc[...] = jnp.zeros_like(acc)

        def sweep_tile(i, carry):
            cols = pl.ds(pl.multiple_of(i * word_tile, word_tile), word_tile)
            tile = beta[cols, :]
            mixture = lax.dot_general(theta[it], tile, (((1,), (1,)), ((), ())),
                                      preferred_element_type=F32)
            quotient = (ratio[:, cols].astype(F32) / mixture).astype(BF)
            if last:
                ratio[:, cols] = quotient
            acc[...] += jnp.dot(quotient, tile, preferred_element_type=F32)
            return carry

        lax.fori_loop(0, words // word_tile, sweep_tile, 0)
        if last:
            own = jnp.sum(theta[it].astype(F32) * acc[...], axis=0, keepdims=True)
            tot_out[...] = jnp.broadcast_to(own, eight)
            peers(lambda p: tot_copy(me, p).start(), n, me)
        part_out[it] = acc[...].astype(BF)
        peers(lambda p: part_copy(it, me, p).start(), n, me)
        if last:
            def stats_tile(i, carry):
                cols = pl.ds(pl.multiple_of(i * word_tile, word_tile), word_tile)
                gathered = lax.dot_general(ratio[:, cols], theta[it], (((0,), (0,)), ((), ())),
                                           preferred_element_type=F32)
                weights[cols, :] = jnp.log(beta[cols, :].astype(F32) * gathered + prior_count)
                return carry

            half = words // word_tile // 2
            lax.fori_loop(0, half, stats_tile, 0)
            tot_in[me] = tot_out[...]
            peers(lambda q: tot_copy(q, q).wait_recv(), n, me)
            row_out[...] = sum(tot_in[q] for q in range(n))
            peers(lambda p: row_copy(now, p).start(), slices, now)
            lax.fori_loop(half, words // word_tile, stats_tile, 0)
        part_in[it, me] = part_out[it, rows(me), :]
        peers(lambda q: part_copy(it, q, q).wait_recv(), n, me)
        summed = sum(part_in[it, q].astype(F32) for q in range(n))
        gamma = prior + theta[it, rows(me), :].astype(F32) * summed
        if last:
            topics_ref[...] = gamma
        else:
            theta[it + 1, rows(me), :] = expected_proportions(gamma).astype(BF)
            peers(lambda p: theta_copy(it + 1, me, p, me).start(), n, me)
            peers(lambda q: theta_copy(it + 1, q, q, q).wait_recv(), n, me)

    row_in[now] = row_out[...]
    peers(lambda q: row_copy(q, q).wait_recv(), slices, now)

    chain = chain_ref[...]
    topics = chain.shape[1]
    previous = initial_scale * chain
    gains, factors = [], []
    for t in range(slices):
        totals = row_in[t, 0:1, :]
        noise = obs_ref[...] * (jnp.sum(totals, axis=1, keepdims=True) / (topics * totals))
        predicted = previous + chain
        gain = predicted / (predicted + noise)
        previous = (1.0 - gain) * predicted
        gains.append(gain)
        factors.append(previous / (previous + chain) if t < slices - 1 else jnp.zeros_like(chain))
    share = [None] * slices
    share[-1] = jnp.ones_like(chain)
    for t in range(slices - 2, -1, -1):
        share[t] = (1.0 - factors[t]) + factors[t] * (1.0 - gains[t + 1]) * share[t + 1]

    def mine(per_slice):
        value = per_slice[0]
        for t in range(1, slices):
            value = jnp.where(now == t, per_slice[t], value)
        return value

    gain, factor, left = mine(gains), mine(factors), mine(share)
    all_words = words * n
    offset = jnp.log((row_in[now, 0:1, :] + prior_count * all_words) / all_words)
    keep = 1.0 - gain
    carried = left * keep
    direct = left * gain

    @pl.when(now == 0)
    def _():
        fwd_in[...] = jnp.zeros_like(fwd_in)

    @pl.when(now == slices - 1)
    def _():
        back_in[...] = jnp.zeros_like(back_in)

    pieces = words // chunk

    def piece(i):
        return pl.ds(pl.multiple_of(i * chunk, chunk), chunk)

    def fwd_copy(i):
        return to_tm(fwd_out.at[piece(i), :], fwd_in.at[piece(i), :], fwd_s.at[i], fwd_r.at[i],
                     lax.rem(now + 1, slices))

    def back_copy(i):
        return to_tm(back_out.at[piece(i), :], back_in.at[piece(i), :], back_s.at[i],
                     back_r.at[i], lax.rem(now + slices - 1, slices))

    lag = slices - 1 - 2 * now
    fwd_lag = jnp.maximum(-lag, 0)
    back_lag = jnp.maximum(lag, 0)
    both_lag = jnp.maximum(fwd_lag, back_lag)

    def step(i, carry):
        f, b, s = i - fwd_lag, i - back_lag, i - both_lag

        @pl.when((f >= 0) & (f < pieces))
        def _():
            @pl.when(now > 0)
            def _():
                fwd_copy(f).wait_recv()

            @pl.when(now < slices - 1)
            def _():
                at = piece(f)
                observed = weights[at, :] - offset
                fwd_out[at, :] = (keep * fwd_in[at, :].astype(F32) + gain * observed).astype(BF)
                fwd_copy(f).start()

        @pl.when((b >= 0) & (b < pieces))
        def _():
            @pl.when(now < slices - 1)
            def _():
                back_copy(b).wait_recv()

            @pl.when(now > 0)
            def _():
                at = piece(b)
                observed = weights[at, :] - offset
                back_out[at, :] = (factor * back_in[at, :].astype(F32)
                                   + direct * observed).astype(BF)
                back_copy(b).start()

        @pl.when((s >= 0) & (s < pieces))
        def _():
            at = piece(s)
            smooth_ref[at, :] = (carried * fwd_in[at, :].astype(F32)
                                 + direct * (weights[at, :] - offset)
                                 + factor * back_in[at, :].astype(F32))
        return carry

    lax.fori_loop(0, pieces + slices - 1, step, 0)

    peers(lambda p: stat_copy(me, p).wait_send(), n, me)
    peers(lambda p: cnt_copy(me, p).wait_send(), n, me)
    peers(lambda p: tot_copy(me, p).wait_send(), n, me)
    peers(lambda p: row_copy(now, p).wait_send(), slices, now)
    for it in range(ITERS_E):
        peers(lambda p: theta_copy(it, me, p, me).wait_send(), n, me)
        peers(lambda p: part_copy(it, me, p).wait_send(), n, me)

    def drain(i, carry):
        @pl.when(now < slices - 1)
        def _():
            fwd_copy(i).wait_send()

        @pl.when(now > 0)
        def _():
            back_copy(i).wait_send()
        return carry

    lax.fori_loop(0, pieces, drain, 0)


def body(counts, topic_means, doc_topics_init, dirichlet_prior, chain_var, obs_noise):
    n = lax.axis_size("docs")
    slices = lax.axis_size("tm")
    docs = counts.shape[1]
    words, topics = topic_means.shape[1:]
    every = docs * n
    word_tile = min(512, words // 2)
    chunk = max(words // 8, 16)
    pieces = words // chunk
    dma = pltpu.SemaphoreType.DMA
    vmem = pl.BlockSpec(memory_space=pltpu.VMEM)
    smoothed, doc_topics = pl.pallas_call(
        functools.partial(round_kernel, n, slices, word_tile, chunk),
        out_shape=(jax.ShapeDtypeStruct((words, topics), F32),
                   jax.ShapeDtypeStruct((docs, topics), F32)),
        in_specs=[pl.BlockSpec(memory_space=pl.ANY)] + [vmem] * 5,
        out_specs=(vmem, vmem),
        scratch_shapes=[
            pltpu.VMEM((n, docs, words), jnp.int32),
            pltpu.VMEM((n, docs, words), BF),
            pltpu.VMEM((every, words), BF),
            pltpu.VMEM((words, topics), F32),
            pltpu.VMEM((words, topics), BF),
            pltpu.VMEM((ITERS_E, every, topics), BF),
            pltpu.VMEM((every, topics), F32),
            pltpu.VMEM((ITERS_E, every, topics), BF),
            pltpu.VMEM((ITERS_E, n, docs, topics), BF),
            pltpu.VMEM((2, 8, topics), F32),
            pltpu.VMEM((n, 2, 8, topics), F32),
            pltpu.VMEM((8, topics), F32),
            pltpu.VMEM((n, 8, topics), F32),
            pltpu.VMEM((8, topics), F32),
            pltpu.VMEM((slices, 8, topics), F32),
            pltpu.VMEM((words, topics), BF),
            pltpu.VMEM((words, topics), BF),
            pltpu.VMEM((words, topics), BF),
            pltpu.VMEM((words, topics), BF),
            dma((n,)),
            dma((n,)), dma((n,)),
            dma((ITERS_E, n)), dma((ITERS_E, n)),
            dma((ITERS_E, n)), dma((ITERS_E, n)),
            dma((n,)), dma((n,)),
            dma((n,)), dma((n,)),
            dma((slices,)), dma((slices,)),
            dma((pieces,)), dma((pieces,)),
            dma((pieces,)), dma((pieces,)),
        ],
        compiler_params=pltpu.CompilerParams(
            collective_id=0, has_side_effects=True, vmem_limit_bytes=58 * 1024 * 1024),
    )(counts[0], topic_means[0], doc_topics_init[0], dirichlet_prior[None], chain_var[None],
      obs_noise[None])
    return smoothed[None], doc_topics[None]


def solution(mesh):
    in_specs = (P("tm", "docs", None), P("tm", "docs", None), P("tm", "docs", None), P(), P(), P())
    out_specs = (P("tm", "docs", None), P("tm", "docs", None))
    return jax.shard_map(body, mesh=mesh, in_specs=in_specs, out_specs=out_specs, check_vma=False)
```

time: 403 us -> 149 us (0.37)
  waiting for transfers between devices: 238 us -> 0 us
  Pallas kernels: 0 us -> 145 us
  blocking collectives: 66.5 us -> 0 us
  matrix products: 61.5 us -> 0 us
  other arithmetic: 19.6 us -> 0 us
  between operations: 13.9 us -> 0.65 us
    all_gather x3 -> x0, waiting for transfers between devices: 214 us -> none  [the longest x1 80.6 us: body(): lax.all_gather(forward_term[None].astype(jnp.bfloat16), 'tm', axis=0, til...]
    pallas_call x0 -> x1, Pallas kernels: none -> 145 us  [body(): pl.pallas_call(functools.partial(round_kernel, n, slices, word_tile, chun...]
    dot_general x6 -> x0, matrix products: 61.5 us -> none  [the longest x4 45 us: body(): jnp.dot(ratios, beta_full, preferred_element_type=jnp.float32)]
    psum x2 -> x0, blocking collectives: 51.3 us -> none  [the longest x1 39.6 us: body(): totals = lax.psum(placed, ('tm', 'docs'))]
    reduce_scatter x1 -> x0, waiting for transfers between devices: 24 us -> none  [body(): lax.psum_scatter((beta_full.astype(jnp.float32) * lax.dot_general(ratios,...]
    pmax x1 -> x0, blocking collectives: 15.1 us -> none  [body(): column_peak = lax.pmax(local_peak, 'docs')]
    dot_general x2 -> x0, other arithmetic: 6.58 us -> none  [body(): jnp.einsum('rk,rwk->wk', weight, shard_piece)]
    convert_element_type x5 -> x0, other arithmetic: 5.59 us -> none  [the longest x1 2.68 us: body(): forward_term[None].astype(jnp.bfloat16)]
  transfers between devices with their start and end apart: 4 -> 0, of which waited for: 4 -> 0; matrix products, arithmetic and copies ran while one was open for 2% -> 0% of each run, Pallas kernels for 0% -> 0%
where the time goes in v1:
time: 149 us
  Pallas kernels  145 us (97%)
  local copies, waits for them, and re-layouts  3.67 us (2%)
    pallas_call x1, Pallas kernels, body(): pl.pallas_call(functools.partial(round_kernel, n, slices, word_tile, chun...  145 us
    unnamed x4, local copies, waits for them, and re-layouts  3.67 us

profile of v1, /device:TPU:0, one launch (start us, length us, event | category | flops | bytes accessed | tf_op | source)
XLA Modules:
  0.0 149.1 jit_solution(14077155314343955940)
XLA Ops:
  0.6 144.8 %shard_map.77 = (f32[4096,128]{1,0:T(8,128)}, f32[64,128]{1,0:T(8,128)}) custom-call(s32[64,32768]{1,0:T(8,128)} %bitcast.8, f32[4096,128]{1,0:T(8,128)} %bitcast.10, f32[64,128]{1,0:T(8,128)} %bitcast.11, f32[1,128]{1,0:T(1,128)} %bitcast.13, f32[1,128]{1,0:T(1,128)} %bitcast.14, f32[1,128]{1,0:T(1,128)} %bitcast.15), custom_call_target="tpu_custom_call" | custom-call | tf_op jit(solution)/shard_map/pallas_call | solution.py:306
  145.5 0.0 copy-start
  145.5 3.0 %copy.10 = f32[1,4096,128]{2,1,0:T(8,128)} copy(f32[1,4096,128]{2,1,0:T(8,128)} %bitcast.9) | data formatting | bytes 4194304
  148.5 0.0 copy-done
  148.5 0.6 copy.11
Async XLA Ops:
  145.5 3.1 %copy-start = (f32[64,128]{1,0:T(8,128)S(1)}, f32[64,128]{1,0:T(8,128)}, u32[]{:S(2)}) copy-start(f32[64,128]{1,0:T(8,128)} %get-tuple-element.5) | copy-start | bytes 98308

commit v2 on v1

--- a/solution.py
+++ b/solution.py
@@ -25,7 +25,7 @@
     return jnp.exp(jnp.log(y) - 0.5 * inv - tail - steps)
 
 
-def round_kernel(n, slices, word_tile, chunk, counts_ref, slab_ref, init_ref, prior_ref, chain_ref,
+def round_kernel(n, slices, word_tile, chunk, sizes, plan, counts_ref, slab_ref, init_ref, prior_ref, chain_ref,
                  obs_ref, smooth_ref, topics_ref, raw, outgoing, ratio, weights, beta, theta,
                  acc, part_out, part_in, stat_out, stat_in, tot_out, tot_in, row_out, row_in,
                  fwd_in, back_in, fwd_out, back_out, load_sem, cnt_s, cnt_r, theta_s, theta_r,
@@ -42,8 +42,16 @@
             return carry
         lax.fori_loop(1, size, step, 0)
 
-    def rows(p):
-        return pl.ds(pl.multiple_of(p * docs, docs), docs)
+    starts = [sum(sizes[:g]) for g in range(len(sizes))]
+
+    def rows(g, p):
+        return pl.ds(pl.multiple_of(starts[g] * n + p * sizes[g], 16), sizes[g])
+
+    def members(g):
+        return pl.ds(starts[g] * n, sizes[g] * n)
+
+    def inner(g):
+        return pl.ds(starts[g], sizes[g])
 
     def load(p):
         return pltpu.make_async_copy(
@@ -70,48 +78,60 @@
     peers(lambda p: pl.semaphore_signal(barrier, inc=1, device_id={"tm": p},
                                         device_id_type=MESH), slices, now)
 
+    def theta_copy(g, it, src_block, p, r):
+        block = theta.at[it, rows(g, src_block), :]
+        return to_docs(block, block, theta_s.at[g, it, p], theta_r.at[g, it, r], p)
+
+    def stat_copy(src_block, p):
+        return to_docs(stat_out, stat_in.at[src_block], stat_s.at[p], stat_r.at[src_block], p)
+
+    def cnt_copy(g, src_block, p):
+        return to_docs(outgoing.at[p, inner(g), :], ratio.at[rows(g, src_block), :],
+                       cnt_s.at[g, p], cnt_r.at[g, src_block], p)
+
+    def part_copy(g, it, src_block, p):
+        return to_docs(part_out.at[it, rows(g, p), :], part_in.at[it, src_block, inner(g), :],
+                       part_s.at[g, it, p], part_r.at[g, it, src_block], p)
+
+    def tot_copy(src_block, p):
+        return to_docs(tot_out, tot_in.at[src_block], tot_s.at[p], tot_r.at[src_block], p)
+
+    def row_copy(src_block, p):
+        return to_tm(row_out, row_in.at[src_block], row_s.at[p], row_r.at[src_block], p)
+
+    groups = range(len(sizes))
+    pl.semaphore_wait(barrier, n - 1 + slices - 1)
+
+    def send_first(p):
+        load(p).wait()
+        outgoing[p, inner(0), :] = raw[p, inner(0), :].astype(F32).astype(BF)
+        cnt_copy(0, me, p).start()
+
+    peers(send_first, n, me)
+
     first = expected_proportions(init_ref[...]).astype(BF)
-    theta[0, rows(me), :] = first
+    for g in groups:
+        theta[0, rows(g, me), :] = first[starts[g]:starts[g] + sizes[g]]
     peak = jnp.max(slab_ref[...], axis=0, keepdims=True)
     weights[...] = jnp.exp(slab_ref[...] - peak)
     mass = jnp.sum(weights[...], axis=0, keepdims=True)
     eight = (8, peak.shape[1])
     stat_out[0] = jnp.broadcast_to(peak, eight)
     stat_out[1] = jnp.broadcast_to(mass, eight)
-    pl.semaphore_wait(barrier, n - 1 + slices - 1)
-
-    def theta_copy(it, src_block, p, r):
-        block = theta.at[it, rows(src_block), :]
-        return to_docs(block, block, theta_s.at[it, p], theta_r.at[it, r], p)
-
-    def stat_copy(src_block, p):
-        return to_docs(stat_out, stat_in.at[src_block], stat_s.at[p], stat_r.at[src_block], p)
-
-    def cnt_copy(src_block, p):
-        return to_docs(outgoing.at[p], ratio.at[rows(src_block), :], cnt_s.at[p],
-                       cnt_r.at[src_block], p)
-
-    def part_copy(it, src_block, p):
-        return to_docs(part_out.at[it, rows(p), :], part_in.at[it, src_block],
-                       part_s.at[it, p], part_r.at[it, src_block], p)
-
-    def tot_copy(src_block, p):
-        return to_docs(tot_out, tot_in.at[src_block], tot_s.at[p], tot_r.at[src_block], p)
-
-    def row_copy(src_block, p):
-        return to_tm(row_out, row_in.at[src_block], row_s.at[p], row_r.at[src_block], p)
-
     peers(lambda p: stat_copy(me, p).start(), n, me)
-    peers(lambda p: theta_copy(0, me, p, me).start(), n, me)
-
-    def send_counts(p):
-        load(p).wait()
-        outgoing[p] = raw[p].astype(F32).astype(BF)
-        cnt_copy(me, p).start()
-
-    peers(send_counts, n, me)
+    for g in groups:
+        peers(lambda p: theta_copy(g, 0, me, p, me).start(), n, me)
+
     load(me).wait()
-    ratio[rows(me), :] = raw[me].astype(F32).astype(BF)
+    for g in groups:
+        ratio[rows(g, me), :] = raw[me, inner(g), :].astype(F32).astype(BF)
+    for g in groups[1:]:
+        def send_later(p):
+            outgoing[p, inner(g), :] = raw[p, inner(g), :].astype(F32).astype(BF)
+            cnt_copy(g - 1, me, p).wait_send()
+            cnt_copy(g, me, p).start()
+
+        peers(send_later, n, me)
 
     stat_in[me] = stat_out[...]
     peers(lambda q: stat_copy(q, q).wait_recv(), n, me)
@@ -120,57 +140,82 @@
     total_mass = sum(stat_in[q, 1, 0:1, :] * jnp.exp(all_peaks[q] - top) for q in range(n))
     beta[...] = (weights[...] * (jnp.exp(peak - top) / total_mass)).astype(BF)
 
-    peers(lambda q: theta_copy(0, q, q, q).wait_recv(), n, me)
-    peers(lambda q: cnt_copy(q, q).wait_recv(), n, me)
-
     prior = prior_ref[...]
-    for it in range(ITERS_E):
-        last = it == ITERS_E - 1
-        acc[...] = jnp.zeros_like(acc)
+    last = ITERS_E - 1
+    tiles = words // word_tile
+
+    def tile_columns(i):
+        return pl.ds(pl.multiple_of(i * word_tile, word_tile), word_tile)
+
+    def sweep(g, it):
+        peers(lambda q: theta_copy(g, it, q, q, q).wait_recv(), n, me)
+        if it == 0:
+            peers(lambda q: cnt_copy(g, q, q).wait_recv(), n, me)
+        own_rows = members(g)
+        acc[own_rows, :] = jnp.zeros((sizes[g] * n, acc.shape[1]), F32)
 
         def sweep_tile(i, carry):
-            cols = pl.ds(pl.multiple_of(i * word_tile, word_tile), word_tile)
+            cols = tile_columns(i)
             tile = beta[cols, :]
-            mixture = lax.dot_general(theta[it], tile, (((1,), (1,)), ((), ())),
+            mixture = lax.dot_general(theta[it, own_rows, :], tile, (((1,), (1,)), ((), ())),
                                       preferred_element_type=F32)
-            quotient = (ratio[:, cols].astype(F32) / mixture).astype(BF)
-            if last:
-                ratio[:, cols] = quotient
-            acc[...] += jnp.dot(quotient, tile, preferred_element_type=F32)
+            inverse = pl.reciprocal(mixture, approx=True)
+            inverse = inverse * (2.0 - mixture * inverse)
+            quotient = (ratio[own_rows, cols].astype(F32) * inverse).astype(BF)
+            if it == last:
+                ratio[own_rows, cols] = quotient
+            acc[own_rows, :] += jnp.dot(quotient, tile, preferred_element_type=F32)
             return carry
 
-        lax.fori_loop(0, words // word_tile, sweep_tile, 0)
-        if last:
-            own = jnp.sum(theta[it].astype(F32) * acc[...], axis=0, keepdims=True)
-            tot_out[...] = jnp.broadcast_to(own, eight)
-            peers(lambda p: tot_copy(me, p).start(), n, me)
-        part_out[it] = acc[...].astype(BF)
-        peers(lambda p: part_copy(it, me, p).start(), n, me)
-        if last:
-            def stats_tile(i, carry):
-                cols = pl.ds(pl.multiple_of(i * word_tile, word_tile), word_tile)
-                gathered = lax.dot_general(ratio[:, cols], theta[it], (((0,), (0,)), ((), ())),
-                                           preferred_element_type=F32)
-                weights[cols, :] = jnp.log(beta[cols, :].astype(F32) * gathered + prior_count)
-                return carry
-
-            half = words // word_tile // 2
-            lax.fori_loop(0, half, stats_tile, 0)
-            tot_in[me] = tot_out[...]
-            peers(lambda q: tot_copy(q, q).wait_recv(), n, me)
-            row_out[...] = sum(tot_in[q] for q in range(n))
-            peers(lambda p: row_copy(now, p).start(), slices, now)
-            lax.fori_loop(half, words // word_tile, stats_tile, 0)
-        part_in[it, me] = part_out[it, rows(me), :]
-        peers(lambda q: part_copy(it, q, q).wait_recv(), n, me)
-        summed = sum(part_in[it, q].astype(F32) for q in range(n))
-        gamma = prior + theta[it, rows(me), :].astype(F32) * summed
-        if last:
-            topics_ref[...] = gamma
+        lax.fori_loop(0, tiles, sweep_tile, 0)
+        part_out[it, own_rows, :] = acc[own_rows, :].astype(BF)
+        if not (it == last and g == groups[-1]):
+            peers(lambda p: part_copy(g, it, me, p).start(), n, me)
+
+    def settle(g, it):
+        part_in[it, me, inner(g), :] = part_out[it, rows(g, me), :]
+        peers(lambda q: part_copy(g, it, q, q).wait_recv(), n, me)
+        summed = sum(part_in[it, q, inner(g), :].astype(F32) for q in range(n))
+        gamma = prior + theta[it, rows(g, me), :].astype(F32) * summed
+        if it == last:
+            topics_ref[inner(g), :] = gamma
         else:
-            theta[it + 1, rows(me), :] = expected_proportions(gamma).astype(BF)
-            peers(lambda p: theta_copy(it + 1, me, p, me).start(), n, me)
-            peers(lambda q: theta_copy(it + 1, q, q, q).wait_recv(), n, me)
+            theta[it + 1, rows(g, me), :] = expected_proportions(gamma).astype(BF)
+            peers(lambda p: theta_copy(g, it + 1, me, p, me).start(), n, me)
+
+    def tally(g, low, high):
+        def stats_tile(i, carry):
+            cols = tile_columns(i)
+            gathered = lax.dot_general(ratio[members(g), cols], theta[last, members(g), :],
+                                       (((0,), (0,)), ((), ())), preferred_element_type=F32)
+            if g > 0:
+                gathered += weights[cols, :]
+            if g == groups[-1]:
+                gathered = jnp.log(beta[cols, :].astype(F32) * gathered + prior_count)
+            weights[cols, :] = gathered
+            return carry
+
+        lax.fori_loop(low, high, stats_tile, 0)
+
+    for what, g, it in plan:
+        if what == "sweep":
+            sweep(g, it)
+        elif what == "settle":
+            settle(g, it)
+        else:
+            tally(g, 0, tiles)
+
+    end = groups[-1]
+    own = jnp.sum(theta[last].astype(F32) * acc[...], axis=0, keepdims=True)
+    tot_out[...] = jnp.broadcast_to(own, eight)
+    peers(lambda p: tot_copy(me, p).start(), n, me)
+    peers(lambda p: part_copy(end, last, me, p).start(), n, me)
+    tally(end, 0, tiles // 2)
+    tot_in[me] = tot_out[...]
+    peers(lambda q: tot_copy(q, q).wait_recv(), n, me)
+    row_out[...] = sum(tot_in[q] for q in range(n))
+    peers(lambda p: row_copy(now, p).start(), slices, now)
+    tally(end, tiles // 2, tiles)
 
     row_in[now] = row_out[...]
     peers(lambda q: row_copy(q, q).wait_recv(), slices, now)
@@ -270,14 +315,16 @@
         return carry
 
     lax.fori_loop(0, pieces + slices - 1, step, 0)
+    settle(end, last)
 
     peers(lambda p: stat_copy(me, p).wait_send(), n, me)
-    peers(lambda p: cnt_copy(me, p).wait_send(), n, me)
+    peers(lambda p: cnt_copy(end, me, p).wait_send(), n, me)
     peers(lambda p: tot_copy(me, p).wait_send(), n, me)
     peers(lambda p: row_copy(now, p).wait_send(), slices, now)
     for it in range(ITERS_E):
-        peers(lambda p: theta_copy(it, me, p, me).wait_send(), n, me)
-        peers(lambda p: part_copy(it, me, p).wait_send(), n, me)
+        for g in groups:
+            peers(lambda p: theta_copy(g, it, me, p, me).wait_send(), n, me)
+            peers(lambda p: part_copy(g, it, me, p).wait_send(), n, me)
 
     def drain(i, carry):
         @pl.when(now < slices - 1)
@@ -299,12 +346,18 @@
     words, topics = topic_means.shape[1:]
     every = docs * n
     word_tile = min(512, words // 2)
-    chunk = max(words // 8, 16)
+    chunk = max(words // 16, 16)
+    sizes = (docs // 2, docs // 2)
+    plan = (("sweep", 0, 0), ("settle", 0, 0), ("sweep", 0, 1), ("settle", 0, 1),
+            ("sweep", 1, 0), ("sweep", 0, 2), ("settle", 1, 0), ("settle", 0, 2),
+            ("sweep", 1, 1), ("sweep", 0, 3), ("settle", 1, 1), ("tally", 0, 3),
+            ("sweep", 1, 2), ("settle", 0, 3), ("settle", 1, 2), ("sweep", 1, 3))
     pieces = words // chunk
+    parts = len(sizes)
     dma = pltpu.SemaphoreType.DMA
     vmem = pl.BlockSpec(memory_space=pltpu.VMEM)
     smoothed, doc_topics = pl.pallas_call(
-        functools.partial(round_kernel, n, slices, word_tile, chunk),
+        functools.partial(round_kernel, n, slices, word_tile, chunk, sizes, plan),
         out_shape=(jax.ShapeDtypeStruct((words, topics), F32),
                    jax.ShapeDtypeStruct((docs, topics), F32)),
         in_specs=[pl.BlockSpec(memory_space=pl.ANY)] + [vmem] * 5,
@@ -330,9 +383,9 @@
             pltpu.VMEM((words, topics), BF),
             pltpu.VMEM((words, topics), BF),
             dma((n,)),
-            dma((n,)), dma((n,)),
-            dma((ITERS_E, n)), dma((ITERS_E, n)),
-            dma((ITERS_E, n)), dma((ITERS_E, n)),
+            dma((parts, n)), dma((parts, n)),
+            dma((parts, ITERS_E, n)), dma((parts, ITERS_E, n)),
+            dma((parts, ITERS_E, n)), dma((parts, ITERS_E, n)),
             dma((n,)), dma((n,)),
             dma((n,)), dma((n,)),
             dma((slices,)), dma((slices,)),

time: 149 us -> 176 us (1.18)
  Pallas kernels: 145 us -> 171 us
    pallas_call x1, Pallas kernels: 145 us -> 171 us  [body(): pl.pallas_call(functools.partial(round_kernel, n, slices, word_tile, chun...]
where the time goes in v2:
time: 176 us; the launch traced here: 175 us
  Pallas kernels  171 us (97%)
  local copies, waits for them, and re-layouts  3.67 us (2%)
    pallas_call x1, Pallas kernels, body(): pl.pallas_call(functools.partial(round_kernel, n, slices, word_tile, chun...  171 us
    unnamed x4, local copies, waits for them, and re-layouts  3.67 us

profile of v2, /device:TPU:0, one launch (start us, length us, event | category | flops | bytes accessed | tf_op | source)
XLA Modules:
  0.0 175.3 jit_solution(17212057033845357929)
XLA Ops:
  0.6 171.0 %shard_map.77 = (f32[4096,128]{1,0:T(8,128)}, f32[64,128]{1,0:T(8,128)}) custom-call(s32[64,32768]{1,0:T(8,128)} %bitcast.8, f32[4096,128]{1,0:T(8,128)} %bitcast.10, f32[64,128]{1,0:T(8,128)} %bitcast.11, f32[1,128]{1,0:T(1,128)} %bitcast.13, f32[1,128]{1,0:T(1,128)} %bitcast.14, f32[1,128]{1,0:T(1,128)} %bitcast.15), custom_call_target="tpu_custom_call" | custom-call | tf_op jit(solution)/shard_map/pallas_call | solution.py:359
  171.6 0.0 copy-start
  171.7 3.0 %copy.10 = f32[1,4096,128]{2,1,0:T(8,128)} copy(f32[1,4096,128]{2,1,0:T(8,128)} %bitcast.9) | data formatting | bytes 4194304
  174.7 0.0 copy-done
  174.7 0.6 copy.11
Async XLA Ops:
  171.6 3.1 %copy-start = (f32[64,128]{1,0:T(8,128)S(1)}, f32[64,128]{1,0:T(8,128)}, u32[]{:S(2)}) copy-start(f32[64,128]{1,0:T(8,128)} %get-tuple-element.5) | copy-start | bytes 98308

commit v3 on v2

--- a/solution.py
+++ b/solution.py
@@ -102,12 +102,13 @@
     groups = range(len(sizes))
     pl.semaphore_wait(barrier, n - 1 + slices - 1)
 
-    def send_first(p):
+    def send_counts(p):
         load(p).wait()
-        outgoing[p, inner(0), :] = raw[p, inner(0), :].astype(F32).astype(BF)
-        cnt_copy(0, me, p).start()
-
-    peers(send_first, n, me)
+        outgoing[p] = raw[p].astype(F32).astype(BF)
+        for g in groups:
+            cnt_copy(g, me, p).start()
+
+    peers(send_counts, n, me)
 
     first = expected_proportions(init_ref[...]).astype(BF)
     for g in groups:
@@ -125,14 +126,6 @@
     load(me).wait()
     for g in groups:
         ratio[rows(g, me), :] = raw[me, inner(g), :].astype(F32).astype(BF)
-    for g in groups[1:]:
-        def send_later(p):
-            outgoing[p, inner(g), :] = raw[p, inner(g), :].astype(F32).astype(BF)
-            cnt_copy(g - 1, me, p).wait_send()
-            cnt_copy(g, me, p).start()
-
-        peers(send_later, n, me)
-
     stat_in[me] = stat_out[...]
     peers(lambda q: stat_copy(q, q).wait_recv(), n, me)
     all_peaks = [stat_in[q, 0, 0:1, :] for q in range(n)]
@@ -198,24 +191,20 @@
         lax.fori_loop(low, high, stats_tile, 0)
 
     for what, g, it in plan:
-        if what == "sweep":
-            sweep(g, it)
-        elif what == "settle":
-            settle(g, it)
-        else:
-            tally(g, 0, tiles)
+        (sweep if what == "sweep" else settle)(g, it)
 
     end = groups[-1]
     own = jnp.sum(theta[last].astype(F32) * acc[...], axis=0, keepdims=True)
     tot_out[...] = jnp.broadcast_to(own, eight)
     peers(lambda p: tot_copy(me, p).start(), n, me)
     peers(lambda p: part_copy(end, last, me, p).start(), n, me)
-    tally(end, 0, tiles // 2)
+    for g in groups[:-1]:
+        tally(g, 0, tiles)
     tot_in[me] = tot_out[...]
     peers(lambda q: tot_copy(q, q).wait_recv(), n, me)
     row_out[...] = sum(tot_in[q] for q in range(n))
     peers(lambda p: row_copy(now, p).start(), slices, now)
-    tally(end, tiles // 2, tiles)
+    tally(end, 0, tiles)
 
     row_in[now] = row_out[...]
     peers(lambda q: row_copy(q, q).wait_recv(), slices, now)
@@ -315,10 +304,12 @@
         return carry
 
     lax.fori_loop(0, pieces + slices - 1, step, 0)
-    settle(end, last)
+    for g in groups:
+        settle(g, last)
 
     peers(lambda p: stat_copy(me, p).wait_send(), n, me)
-    peers(lambda p: cnt_copy(end, me, p).wait_send(), n, me)
+    for g in groups:
+        peers(lambda p: cnt_copy(g, me, p).wait_send(), n, me)
     peers(lambda p: tot_copy(me, p).wait_send(), n, me)
     peers(lambda p: row_copy(now, p).wait_send(), slices, now)
     for it in range(ITERS_E):
@@ -348,10 +339,8 @@
     word_tile = min(512, words // 2)
     chunk = max(words // 16, 16)
     sizes = (docs // 2, docs // 2)
-    plan = (("sweep", 0, 0), ("settle", 0, 0), ("sweep", 0, 1), ("settle", 0, 1),
-            ("sweep", 1, 0), ("sweep", 0, 2), ("settle", 1, 0), ("settle", 0, 2),
-            ("sweep", 1, 1), ("sweep", 0, 3), ("settle", 1, 1), ("tally", 0, 3),
-            ("sweep", 1, 2), ("settle", 0, 3), ("settle", 1, 2), ("sweep", 1, 3))
+    plan = tuple((what, g, it) for it in range(ITERS_E) for what in ("sweep", "settle")
+                 for g in range(len(sizes)) if what == "sweep" or it < ITERS_E - 1)
     pieces = words // chunk
     parts = len(sizes)
     dma = pltpu.SemaphoreType.DMA

time: 176 us -> 168 us (0.955)
  Pallas kernels: 171 us -> 164 us
    pallas_call x1, Pallas kernels: 171 us -> 164 us  [body(): pl.pallas_call(functools.partial(round_kernel, n, slices, word_tile, chun...]
where the time goes in v3:
time: 168 us
  Pallas kernels  164 us (98%)
  local copies, waits for them, and re-layouts  3.67 us (2%)
    pallas_call x1, Pallas kernels, body(): pl.pallas_call(functools.partial(round_kernel, n, slices, word_tile, chun...  164 us
    unnamed x4, local copies, waits for them, and re-layouts  3.67 us

profile of v3, /device:TPU:0, one launch (start us, length us, event | category | flops | bytes accessed | tf_op | source)
XLA Modules:
  0.0 168.3 jit_solution(2363897554631968985)
XLA Ops:
  0.6 164.0 %shard_map.77 = (f32[4096,128]{1,0:T(8,128)}, f32[64,128]{1,0:T(8,128)}) custom-call(s32[64,32768]{1,0:T(8,128)} %bitcast.8, f32[4096,128]{1,0:T(8,128)} %bitcast.10, f32[64,128]{1,0:T(8,128)} %bitcast.11, f32[1,128]{1,0:T(1,128)} %bitcast.13, f32[1,128]{1,0:T(1,128)} %bitcast.14, f32[1,128]{1,0:T(1,128)} %bitcast.15), custom_call_target="tpu_custom_call" | custom-call | tf_op jit(solution)/shard_map/pallas_call | solution.py:348
  164.6 0.0 copy-start
  164.6 3.0 %copy.10 = f32[1,4096,128]{2,1,0:T(8,128)} copy(f32[1,4096,128]{2,1,0:T(8,128)} %bitcast.9) | data formatting | bytes 4194304
  167.7 0.0 copy-done
  167.7 0.6 copy.11
Async XLA Ops:
  164.6 3.1 %copy-start = (f32[64,128]{1,0:T(8,128)S(1)}, f32[64,128]{1,0:T(8,128)}, u32[]{:S(2)}) copy-start(f32[64,128]{1,0:T(8,128)} %get-tuple-element.5) | copy-start | bytes 98308

commit v4 on v3

--- a/solution.py
+++ b/solution.py
@@ -160,7 +160,7 @@
             acc[own_rows, :] += jnp.dot(quotient, tile, preferred_element_type=F32)
             return carry
 
-        lax.fori_loop(0, tiles, sweep_tile, 0)
+        lax.fori_loop(0, tiles, sweep_tile, 0, unroll=2)
         part_out[it, own_rows, :] = acc[own_rows, :].astype(BF)
         if not (it == last and g == groups[-1]):
             peers(lambda p: part_copy(g, it, me, p).start(), n, me)
@@ -337,8 +337,8 @@
     words, topics = topic_means.shape[1:]
     every = docs * n
     word_tile = min(512, words // 2)
-    chunk = max(words // 16, 16)
-    sizes = (docs // 2, docs // 2)
+    chunk = max(words // 8, 16)
+    sizes = (docs,)
     plan = tuple((what, g, it) for it in range(ITERS_E) for what in ("sweep", "settle")
                  for g in range(len(sizes)) if what == "sweep" or it < ITERS_E - 1)
     pieces = words // chunk

time: 168 us -> 150 us (0.89)
  Pallas kernels: 164 us -> 145 us
    pallas_call x1, Pallas kernels: 164 us -> 145 us  [body(): pl.pallas_call(functools.partial(round_kernel, n, slices, word_tile, chun...]
where the time goes in v4:
time: 150 us; the launch traced here: 149 us
  Pallas kernels  145 us (97%)
  local copies, waits for them, and re-layouts  3.67 us (2%)
    pallas_call x1, Pallas kernels, body(): pl.pallas_call(functools.partial(round_kernel, n, slices, word_tile, chun...  145 us
    unnamed x4, local copies, waits for them, and re-layouts  3.67 us

profile of v4, /device:TPU:0, one launch (start us, length us, event | category | flops | bytes accessed | tf_op | source)
XLA Modules:
  0.0 149.4 jit_solution(9746070046833228169)
XLA Ops:
  0.6 145.0 %shard_map.77 = (f32[4096,128]{1,0:T(8,128)}, f32[64,128]{1,0:T(8,128)}) custom-call(s32[64,32768]{1,0:T(8,128)} %bitcast.8, f32[4096,128]{1,0:T(8,128)} %bitcast.10, f32[64,128]{1,0:T(8,128)} %bitcast.11, f32[1,128]{1,0:T(1,128)} %bitcast.13, f32[1,128]{1,0:T(1,128)} %bitcast.14, f32[1,128]{1,0:T(1,128)} %bitcast.15), custom_call_target="tpu_custom_call" | custom-call | tf_op jit(solution)/shard_map/pallas_call | solution.py:348
  145.7 0.0 copy-start
  145.7 3.0 %copy.10 = f32[1,4096,128]{2,1,0:T(8,128)} copy(f32[1,4096,128]{2,1,0:T(8,128)} %bitcast.9) | data formatting | bytes 4194304
  148.7 0.0 copy-done
  148.7 0.6 copy.11
Async XLA Ops:
  145.7 3.1 %copy-start = (f32[64,128]{1,0:T(8,128)S(1)}, f32[64,128]{1,0:T(8,128)}, u32[]{:S(2)}) copy-start(f32[64,128]{1,0:T(8,128)} %get-tuple-element.5) | copy-start | bytes 98308

commit v5 on v1

--- a/solution.py
+++ b/solution.py
@@ -37,13 +37,16 @@
     now = lax.axis_index("tm")
 
     def peers(fn, size, own):
-        def step(m, carry):
-            fn(lax.rem(own + m, size))
-            return carry
-        lax.fori_loop(1, size, step, 0)
+        for m in range(1, size):
+            fn(m, lax.rem(own + m, size))
+
+    def wait_bytes(ref, sem):
+        pltpu.make_async_copy(ref, ref, sem).wait()
 
     def rows(p):
         return pl.ds(pl.multiple_of(p * docs, docs), docs)
+
+    others = pl.ds(0, (n - 1) * docs)
 
     def load(p):
         return pltpu.make_async_copy(
@@ -65,115 +68,115 @@
     lax.fori_loop(0, n, load_all, 0)
 
     barrier = pltpu.get_barrier_semaphore()
-    peers(lambda p: pl.semaphore_signal(barrier, inc=1, device_id={"docs": p},
-                                        device_id_type=MESH), n, me)
-    peers(lambda p: pl.semaphore_signal(barrier, inc=1, device_id={"tm": p},
-                                        device_id_type=MESH), slices, now)
-
-    first = expected_proportions(init_ref[...]).astype(BF)
-    theta[0, rows(me), :] = first
+    peers(lambda m, p: pl.semaphore_signal(barrier, inc=1, device_id={"docs": p},
+                                           device_id_type=MESH), n, me)
+    peers(lambda m, p: pl.semaphore_signal(barrier, inc=1, device_id={"tm": p},
+                                           device_id_type=MESH), slices, now)
+
+    def send_theta(it):
+        block = theta.at[it, rows(me), :]
+        peers(lambda m, p: to_docs(block, block, theta_s.at[it], theta_r.at[it], p).start(), n, me)
+
+    def send_parts(it):
+        peers(lambda m, p: to_docs(part_out.at[it, rows(p), :], part_in.at[it, m - 1],
+                                   part_s.at[it], part_r.at[it], p).start(), n, me)
+
+    pl.semaphore_wait(barrier, n - 1 + slices - 1)
+
+    def send_counts(m, carry):
+        p = lax.rem(me + m, n)
+        load(p).wait()
+        outgoing[m - 1] = raw[p].astype(F32).astype(BF)
+        to_docs(outgoing.at[m - 1], ratio.at[rows(me), :], cnt_s.at[0], cnt_r.at[0], p).start()
+        return carry
+
+    lax.fori_loop(1, n, send_counts, 0)
+
+    theta[0, rows(me), :] = expected_proportions(init_ref[...]).astype(BF)
     peak = jnp.max(slab_ref[...], axis=0, keepdims=True)
     weights[...] = jnp.exp(slab_ref[...] - peak)
     mass = jnp.sum(weights[...], axis=0, keepdims=True)
     eight = (8, peak.shape[1])
     stat_out[0] = jnp.broadcast_to(peak, eight)
     stat_out[1] = jnp.broadcast_to(mass, eight)
-    pl.semaphore_wait(barrier, n - 1 + slices - 1)
-
-    def theta_copy(it, src_block, p, r):
-        block = theta.at[it, rows(src_block), :]
-        return to_docs(block, block, theta_s.at[it, p], theta_r.at[it, r], p)
-
-    def stat_copy(src_block, p):
-        return to_docs(stat_out, stat_in.at[src_block], stat_s.at[p], stat_r.at[src_block], p)
-
-    def cnt_copy(src_block, p):
-        return to_docs(outgoing.at[p], ratio.at[rows(src_block), :], cnt_s.at[p],
-                       cnt_r.at[src_block], p)
-
-    def part_copy(it, src_block, p):
-        return to_docs(part_out.at[it, rows(p), :], part_in.at[it, src_block],
-                       part_s.at[it, p], part_r.at[it, src_block], p)
-
-    def tot_copy(src_block, p):
-        return to_docs(tot_out, tot_in.at[src_block], tot_s.at[p], tot_r.at[src_block], p)
-
-    def row_copy(src_block, p):
-        return to_tm(row_out, row_in.at[src_block], row_s.at[p], row_r.at[src_block], p)
-
-    peers(lambda p: stat_copy(me, p).start(), n, me)
-    peers(lambda p: theta_copy(0, me, p, me).start(), n, me)
-
-    def send_counts(p):
-        load(p).wait()
-        outgoing[p] = raw[p].astype(F32).astype(BF)
-        cnt_copy(me, p).start()
-
-    peers(send_counts, n, me)
+    peers(lambda m, p: to_docs(stat_out, stat_in.at[m - 1], stat_s.at[0], stat_r.at[0], p).start(),
+          n, me)
+    send_theta(0)
+
     load(me).wait()
     ratio[rows(me), :] = raw[me].astype(F32).astype(BF)
 
-    stat_in[me] = stat_out[...]
-    peers(lambda q: stat_copy(q, q).wait_recv(), n, me)
+    stat_in[n - 1] = stat_out[...]
+    wait_bytes(stat_in.at[pl.ds(0, n - 1)], stat_r.at[0])
     all_peaks = [stat_in[q, 0, 0:1, :] for q in range(n)]
     top = functools.reduce(jnp.maximum, all_peaks)
     total_mass = sum(stat_in[q, 1, 0:1, :] * jnp.exp(all_peaks[q] - top) for q in range(n))
     beta[...] = (weights[...] * (jnp.exp(peak - top) / total_mass)).astype(BF)
 
-    peers(lambda q: theta_copy(0, q, q, q).wait_recv(), n, me)
-    peers(lambda q: cnt_copy(q, q).wait_recv(), n, me)
-
     prior = prior_ref[...]
-    for it in range(ITERS_E):
-        last = it == ITERS_E - 1
+    last = ITERS_E - 1
+    tiles = words // word_tile
+
+    def tile_columns(i):
+        return pl.ds(pl.multiple_of(i * word_tile, word_tile), word_tile)
+
+    def sweep(it):
+        wait_bytes(theta.at[it, others, :], theta_r.at[it])
+        if it == 0:
+            wait_bytes(ratio.at[others, :], cnt_r.at[0])
         acc[...] = jnp.zeros_like(acc)
 
         def sweep_tile(i, carry):
-            cols = pl.ds(pl.multiple_of(i * word_tile, word_tile), word_tile)
+            cols = tile_columns(i)
             tile = beta[cols, :]
             mixture = lax.dot_general(theta[it], tile, (((1,), (1,)), ((), ())),
                                       preferred_element_type=F32)
-            quotient = (ratio[:, cols].astype(F32) / mixture).astype(BF)
-            if last:
+            inverse = pl.reciprocal(mixture, approx=True)
+            inverse = inverse * (2.0 - mixture * inverse)
+            quotient = (ratio[:, cols].astype(F32) * inverse).astype(BF)
+            if it == last:
                 ratio[:, cols] = quotient
             acc[...] += jnp.dot(quotient, tile, preferred_element_type=F32)
             return carry
 
-        lax.fori_loop(0, words // word_tile, sweep_tile, 0)
-        if last:
-            own = jnp.sum(theta[it].astype(F32) * acc[...], axis=0, keepdims=True)
-            tot_out[...] = jnp.broadcast_to(own, eight)
-            peers(lambda p: tot_copy(me, p).start(), n, me)
+        lax.fori_loop(0, tiles, sweep_tile, 0, unroll=2)
         part_out[it] = acc[...].astype(BF)
-        peers(lambda p: part_copy(it, me, p).start(), n, me)
-        if last:
-            def stats_tile(i, carry):
-                cols = pl.ds(pl.multiple_of(i * word_tile, word_tile), word_tile)
-                gathered = lax.dot_general(ratio[:, cols], theta[it], (((0,), (0,)), ((), ())),
-                                           preferred_element_type=F32)
-                weights[cols, :] = jnp.log(beta[cols, :].astype(F32) * gathered + prior_count)
-                return carry
-
-            half = words // word_tile // 2
-            lax.fori_loop(0, half, stats_tile, 0)
-            tot_in[me] = tot_out[...]
-            peers(lambda q: tot_copy(q, q).wait_recv(), n, me)
-            row_out[...] = sum(tot_in[q] for q in range(n))
-            peers(lambda p: row_copy(now, p).start(), slices, now)
-            lax.fori_loop(half, words // word_tile, stats_tile, 0)
-        part_in[it, me] = part_out[it, rows(me), :]
-        peers(lambda q: part_copy(it, q, q).wait_recv(), n, me)
+
+    def settle(it):
+        part_in[it, n - 1] = part_out[it, rows(me), :]
+        wait_bytes(part_in.at[it, pl.ds(0, n - 1)], part_r.at[it])
         summed = sum(part_in[it, q].astype(F32) for q in range(n))
-        gamma = prior + theta[it, rows(me), :].astype(F32) * summed
-        if last:
-            topics_ref[...] = gamma
-        else:
-            theta[it + 1, rows(me), :] = expected_proportions(gamma).astype(BF)
-            peers(lambda p: theta_copy(it + 1, me, p, me).start(), n, me)
-            peers(lambda q: theta_copy(it + 1, q, q, q).wait_recv(), n, me)
+        return prior + theta[it, rows(me), :].astype(F32) * summed
+
+    def stats_tile(i, carry):
+        cols = tile_columns(i)
+        gathered = lax.dot_general(ratio[:, cols], theta[last], (((0,), (0,)), ((), ())),
+                                   preferred_element_type=F32)
+        weights[cols, :] = jnp.log(beta[cols, :].astype(F32) * gathered + prior_count)
+        return carry
+
+    for it in range(last):
+        sweep(it)
+        send_parts(it)
+        theta[it + 1, rows(me), :] = expected_proportions(settle(it)).astype(BF)
+        send_theta(it + 1)
+
+    sweep(last)
+    own = jnp.sum(theta[last].astype(F32) * acc[...], axis=0, keepdims=True)
+    tot_out[...] = jnp.broadcast_to(own, eight)
+    peers(lambda m, p: to_docs(tot_out, tot_in.at[m - 1], tot_s.at[0], tot_r.at[0], p).start(),
+          n, me)
+    send_parts(last)
+    lax.fori_loop(0, tiles // 2, stats_tile, 0)
+    tot_in[n - 1] = tot_out[...]
+    wait_bytes(tot_in.at[pl.ds(0, n - 1)], tot_r.at[0])
+    row_out[...] = sum(tot_in[q] for q in range(n))
+    peers(lambda m, p: to_tm(row_out, row_in.at[now], row_s.at[0], row_r.at[0], p).start(),
+          slices, now)
+    lax.fori_loop(tiles // 2, tiles, stats_tile, 0)
 
     row_in[now] = row_out[...]
-    peers(lambda q: row_copy(q, q).wait_recv(), slices, now)
+    wait_bytes(row_in.at[pl.ds(0, slices - 1)], row_r.at[0])
 
     chain = chain_ref[...]
     topics = chain.shape[1]
@@ -226,7 +229,7 @@
         return to_tm(back_out.at[piece(i), :], back_in.at[piece(i), :], back_s.at[i],
                      back_r.at[i], lax.rem(now + slices - 1, slices))
 
-    lag = slices - 1 - 2 * now
+    lag = 2 * (slices - 1 - 2 * now)
     fwd_lag = jnp.maximum(-lag, 0)
     back_lag = jnp.maximum(lag, 0)
     both_lag = jnp.maximum(fwd_lag, back_lag)
@@ -264,20 +267,22 @@
         @pl.when((s >= 0) & (s < pieces))
         def _():
             at = piece(s)
-            smooth_ref[at, :] = (carried * fwd_in[at, :].astype(F32)
-                                 + direct * (weights[at, :] - offset)
-                                 + factor * back_in[at, :].astype(F32))
-        return carry
-
-    lax.fori_loop(0, pieces + slices - 1, step, 0)
-
-    peers(lambda p: stat_copy(me, p).wait_send(), n, me)
-    peers(lambda p: cnt_copy(me, p).wait_send(), n, me)
-    peers(lambda p: tot_copy(me, p).wait_send(), n, me)
-    peers(lambda p: row_copy(now, p).wait_send(), slices, now)
+            smoothed = (carried * fwd_in[at, :].astype(F32)
+                        + direct * (weights[at, :] - offset)
+                        + factor * back_in[at, :].astype(F32))
+            smooth_ref[at, :] = smoothed.astype(BF)
+        return carry
+
+    lax.fori_loop(0, pieces + 2 * (slices - 1), step, 0)
+    topics_ref[...] = settle(last)
+
+    wait_bytes(stat_in.at[pl.ds(0, n - 1)], stat_s.at[0])
+    wait_bytes(ratio.at[others, :], cnt_s.at[0])
+    wait_bytes(tot_in.at[pl.ds(0, n - 1)], tot_s.at[0])
+    wait_bytes(row_in.at[pl.ds(0, slices - 1)], row_s.at[0])
     for it in range(ITERS_E):
-        peers(lambda p: theta_copy(it, me, p, me).wait_send(), n, me)
-        peers(lambda p: part_copy(it, me, p).wait_send(), n, me)
+        wait_bytes(theta.at[it, others, :], theta_s.at[it])
+        wait_bytes(part_in.at[it, pl.ds(0, n - 1)], part_s.at[it])
 
     def drain(i, carry):
         @pl.when(now < slices - 1)
@@ -299,19 +304,19 @@
     words, topics = topic_means.shape[1:]
     every = docs * n
     word_tile = min(512, words // 2)
-    chunk = max(words // 8, 16)
+    chunk = max(words // 16, 16)
     pieces = words // chunk
     dma = pltpu.SemaphoreType.DMA
     vmem = pl.BlockSpec(memory_space=pltpu.VMEM)
     smoothed, doc_topics = pl.pallas_call(
         functools.partial(round_kernel, n, slices, word_tile, chunk),
-        out_shape=(jax.ShapeDtypeStruct((words, topics), F32),
+        out_shape=(jax.ShapeDtypeStruct((words, topics), BF),
                    jax.ShapeDtypeStruct((docs, topics), F32)),
         in_specs=[pl.BlockSpec(memory_space=pl.ANY)] + [vmem] * 5,
         out_specs=(vmem, vmem),
         scratch_shapes=[
             pltpu.VMEM((n, docs, words), jnp.int32),
-            pltpu.VMEM((n, docs, words), BF),
+            pltpu.VMEM((n - 1, docs, words), BF),
             pltpu.VMEM((every, words), BF),
             pltpu.VMEM((words, topics), F32),
             pltpu.VMEM((words, topics), BF),
@@ -330,12 +335,12 @@
             pltpu.VMEM((words, topics), BF),
             pltpu.VMEM((words, topics), BF),
             dma((n,)),
-            dma((n,)), dma((n,)),
-            dma((ITERS_E, n)), dma((ITERS_E, n)),
-            dma((ITERS_E, n)), dma((ITERS_E, n)),
-            dma((n,)), dma((n,)),
-            dma((n,)), dma((n,)),
-            dma((slices,)), dma((slices,)),
+            dma((1,)), dma((1,)),
+            dma((ITERS_E,)), dma((ITERS_E,)),
+            dma((ITERS_E,)), dma((ITERS_E,)),
+            dma((1,)), dma((1,)),
+            dma((1,)), dma((1,)),
+            dma((1,)), dma((1,)),
             dma((pieces,)), dma((pieces,)),
             dma((pieces,)), dma((pieces,)),
         ],
@@ -343,7 +348,7 @@
             collective_id=0, has_side_effects=True, vmem_limit_bytes=58 * 1024 * 1024),
     )(counts[0], topic_means[0], doc_topics_init[0], dirichlet_prior[None], chain_var[None],
       obs_noise[None])
-    return smoothed[None], doc_topics[None]
+    return smoothed.astype(F32)[None], doc_topics[None]
 
 
 def solution(mesh):

time: 149 us -> 141 us (0.946)
  Pallas kernels: 145 us -> 136 us
  local copies, waits for them, and re-layouts: 3.67 us -> 0.62 us
  other arithmetic: 0 us -> 2.68 us
    pallas_call x1, Pallas kernels: 145 us -> 136 us  [body(): pl.pallas_call(functools.partial(round_kernel, n, slices, word_tile, chun...]
    unnamed x4 -> x3, local copies, waits for them, and re-layouts: 3.67 us -> 0.62 us
    broadcast_in_dim x0 -> x1, other arithmetic: none -> 2.68 us  [body(): return (smoothed.astype(F32)[None], doc_topics[None])]
where the time goes in v5:
time: 141 us; the launch traced here: 140 us
  Pallas kernels  136 us (96%)
  other arithmetic  2.68 us (2%)
    pallas_call x1, Pallas kernels, body(): pl.pallas_call(functools.partial(round_kernel, n, slices, word_tile, chun...  136 us

profile of v5, /device:TPU:0, one launch (start us, length us, event | category | flops | bytes accessed | tf_op | source)
XLA Modules:
  0.0 140.4 jit_solution(6299794853355089560)
XLA Ops:
  0.6 136.5 %shard_map.77 = (bf16[4096,128]{1,0:T(8,128)(2,1)}, f32[64,128]{1,0:T(8,128)}) custom-call(s32[64,32768]{1,0:T(8,128)} %bitcast.10, f32[4096,128]{1,0:T(8,128)} %bitcast.11, f32[64,128]{1,0:T(8,128)} %bitcast.12, f32[1,128]{1,0:T(1,128)} %bitcast.14, f32[1,128]{1,0:T(1,128)} %bitcast.15, f32[1,128]{1,0:T(1,128)} %bitcast.16), custom_call_target="tpu_custom_call" | custom-call | tf_op jit(solution)/shard_map/pallas_call | solution.py:311
  137.1 0.0 copy-start
  137.1 2.7 %bitcast_convert_fusion = f32[1,4096,128]{2,1,0:T(8,128)} fusion(bf16[4096,128]{1,0:T(8,128)(2,1)} %get-tuple-element.4), kind=kLoop, calls=%fused_computation | loop fusion | flops 524288 | bytes 3145728 | tf_op jit(solution)/shard_map/broadcast_in_dim | solution.py:351
  139.8 0.0 copy-done
  139.8 0.6 copy.9
Async XLA Ops:
  137.1 2.7 %copy-start = (f32[64,128]{1,0:T(8,128)S(1)}, f32[64,128]{1,0:T(8,128)}, u32[]{:S(2)}) copy-start(f32[64,128]{1,0:T(8,128)} %get-tuple-element.5) | copy-start | bytes 98308

commit v6 on v5

--- a/solution.py
+++ b/solution.py
@@ -25,7 +25,7 @@
     return jnp.exp(jnp.log(y) - 0.5 * inv - tail - steps)
 
 
-def round_kernel(n, slices, word_tile, chunk, counts_ref, slab_ref, init_ref, prior_ref, chain_ref,
+def round_kernel(n, slices, word_tile, chunk, rounds, counts_ref, slab_ref, init_ref, prior_ref, chain_ref,
                  obs_ref, smooth_ref, topics_ref, raw, outgoing, ratio, weights, beta, theta,
                  acc, part_out, part_in, stat_out, stat_in, tot_out, tot_in, row_out, row_in,
                  fwd_in, back_in, fwd_out, back_out, load_sem, cnt_s, cnt_r, theta_s, theta_r,
@@ -83,14 +83,22 @@
 
     pl.semaphore_wait(barrier, n - 1 + slices - 1)
 
-    def send_counts(m, carry):
+    part = docs // rounds
+
+    def send_part(m, r):
+        span = pl.ds(pl.multiple_of(r * part, part), part)
+        there = pl.ds(pl.multiple_of(me * docs + r * part, part), part)
+        to_docs(outgoing.at[m - 1, span, :], ratio.at[there, :], cnt_s.at[0], cnt_r.at[0],
+                lax.rem(me + m, n)).start()
+
+    def first_round(m, carry):
         p = lax.rem(me + m, n)
         load(p).wait()
         outgoing[m - 1] = raw[p].astype(F32).astype(BF)
-        to_docs(outgoing.at[m - 1], ratio.at[rows(me), :], cnt_s.at[0], cnt_r.at[0], p).start()
-        return carry
-
-    lax.fori_loop(1, n, send_counts, 0)
+        send_part(m, 0)
+        return carry
+
+    lax.fori_loop(1, n, first_round, 0)
 
     theta[0, rows(me), :] = expected_proportions(init_ref[...]).astype(BF)
     peak = jnp.max(slab_ref[...], axis=0, keepdims=True)
@@ -103,6 +111,11 @@
           n, me)
     send_theta(0)
 
+    def later_rounds(i, carry):
+        send_part(1 + lax.rem(i, n - 1), 1 + i // (n - 1))
+        return carry
+
+    lax.fori_loop(0, (rounds - 1) * (n - 1), later_rounds, 0)
     load(me).wait()
     ratio[rows(me), :] = raw[me].astype(F32).astype(BF)
 
@@ -133,7 +146,7 @@
                                       preferred_element_type=F32)
             inverse = pl.reciprocal(mixture, approx=True)
             inverse = inverse * (2.0 - mixture * inverse)
-            quotient = (ratio[:, cols].astype(F32) * inverse).astype(BF)
+            quotient = ratio[:, cols] * inverse.astype(BF)
             if it == last:
                 ratio[:, cols] = quotient
             acc[...] += jnp.dot(quotient, tile, preferred_element_type=F32)
@@ -229,7 +242,7 @@
         return to_tm(back_out.at[piece(i), :], back_in.at[piece(i), :], back_s.at[i],
                      back_r.at[i], lax.rem(now + slices - 1, slices))
 
-    lag = 2 * (slices - 1 - 2 * now)
+    lag = 3 * (slices - 1 - 2 * now)
     fwd_lag = jnp.maximum(-lag, 0)
     back_lag = jnp.maximum(lag, 0)
     both_lag = jnp.maximum(fwd_lag, back_lag)
@@ -273,7 +286,7 @@
             smooth_ref[at, :] = smoothed.astype(BF)
         return carry
 
-    lax.fori_loop(0, pieces + 2 * (slices - 1), step, 0)
+    lax.fori_loop(0, pieces + 3 * (slices - 1), step, 0)
     topics_ref[...] = settle(last)
 
     wait_bytes(stat_in.at[pl.ds(0, n - 1)], stat_s.at[0])
@@ -304,12 +317,13 @@
     words, topics = topic_means.shape[1:]
     every = docs * n
     word_tile = min(512, words // 2)
-    chunk = max(words // 16, 16)
+    chunk = max(words // 32, 16)
     pieces = words // chunk
+    rounds = max(min(4, docs // 16), 1)
     dma = pltpu.SemaphoreType.DMA
     vmem = pl.BlockSpec(memory_space=pltpu.VMEM)
     smoothed, doc_topics = pl.pallas_call(
-        functools.partial(round_kernel, n, slices, word_tile, chunk),
+        functools.partial(round_kernel, n, slices, word_tile, chunk, rounds),
         out_shape=(jax.ShapeDtypeStruct((words, topics), BF),
                    jax.ShapeDtypeStruct((docs, topics), F32)),
         in_specs=[pl.BlockSpec(memory_space=pl.ANY)] + [vmem] * 5,

time: 141 us -> 144 us (1.021)
  Pallas kernels: 136 us -> 140 us
    pallas_call x1, Pallas kernels: 136 us -> 140 us  [body(): pl.pallas_call(functools.partial(round_kernel, n, slices, word_tile, chun...]
where the time goes in v6:
time: 144 us
  Pallas kernels  140 us (97%)
  other arithmetic  2.68 us (2%)
    pallas_call x1, Pallas kernels, body(): pl.pallas_call(functools.partial(round_kernel, n, slices, word_tile, chun...  140 us

profile of v6, /device:TPU:0, one launch (start us, length us, event | category | flops | bytes accessed | tf_op | source)
XLA Modules:
  0.0 144.1 jit_solution(5626003520226934944)
XLA Ops:
  0.6 140.2 %shard_map.77 = (bf16[4096,128]{1,0:T(8,128)(2,1)}, f32[64,128]{1,0:T(8,128)}) custom-call(s32[64,32768]{1,0:T(8,128)} %bitcast.10, f32[4096,128]{1,0:T(8,128)} %bitcast.11, f32[64,128]{1,0:T(8,128)} %bitcast.12, f32[1,128]{1,0:T(1,128)} %bitcast.14, f32[1,128]{1,0:T(1,128)} %bitcast.15, f32[1,128]{1,0:T(1,128)} %bitcast.16), custom_call_target="tpu_custom_call" | custom-call | tf_op jit(solution)/shard_map/pallas_call | solution.py:325
  140.8 0.0 copy-start
  140.8 2.7 %bitcast_convert_fusion = f32[1,4096,128]{2,1,0:T(8,128)} fusion(bf16[4096,128]{1,0:T(8,128)(2,1)} %get-tuple-element.4), kind=kLoop, calls=%fused_computation | loop fusion | flops 524288 | bytes 3145728 | tf_op jit(solution)/shard_map/broadcast_in_dim | solution.py:365
  143.5 0.0 copy-done
  143.5 0.6 copy.9
Async XLA Ops:
  140.8 2.7 %copy-start = (f32[64,128]{1,0:T(8,128)S(1)}, f32[64,128]{1,0:T(8,128)}, u32[]{:S(2)}) copy-start(f32[64,128]{1,0:T(8,128)} %get-tuple-element.5) | copy-start | bytes 98308

commit v7 on v6

--- a/solution.py
+++ b/solution.py
@@ -26,7 +26,7 @@
 
 
 def round_kernel(n, slices, word_tile, chunk, rounds, counts_ref, slab_ref, init_ref, prior_ref, chain_ref,
-                 obs_ref, smooth_ref, topics_ref, raw, outgoing, ratio, weights, beta, theta,
+                 obs_ref, smooth_ref, topics_ref, raw, outgoing, ratio, inverse, weights, beta, theta,
                  acc, part_out, part_in, stat_out, stat_in, tot_out, tot_in, row_out, row_in,
                  fwd_in, back_in, fwd_out, back_out, load_sem, cnt_s, cnt_r, theta_s, theta_r,
                  part_s, part_r, stat_s, stat_r, tot_s, tot_r, row_s, row_r, fwd_s, fwd_r,
@@ -135,18 +135,25 @@
 
     def sweep(it):
         wait_bytes(theta.at[it, others, :], theta_r.at[it])
+        def invert(i):
+            mixture = lax.dot_general(theta[it], beta[tile_columns(i), :],
+                                      (((1,), (1,)), ((), ())), preferred_element_type=F32)
+            guess = pl.reciprocal(mixture, approx=True)
+            return (guess * (2.0 - mixture * guess)).astype(BF)
+
         if it == 0:
+            def early(i, carry):
+                inverse[:, tile_columns(i)] = invert(i)
+                return carry
+
+            lax.fori_loop(0, tiles, early, 0)
             wait_bytes(ratio.at[others, :], cnt_r.at[0])
         acc[...] = jnp.zeros_like(acc)
 
         def sweep_tile(i, carry):
             cols = tile_columns(i)
             tile = beta[cols, :]
-            mixture = lax.dot_general(theta[it], tile, (((1,), (1,)), ((), ())),
-                                      preferred_element_type=F32)
-            inverse = pl.reciprocal(mixture, approx=True)
-            inverse = inverse * (2.0 - mixture * inverse)
-            quotient = ratio[:, cols] * inverse.astype(BF)
+            quotient = ratio[:, cols] * (inverse[:, cols] if it == 0 else invert(i))
             if it == last:
                 ratio[:, cols] = quotient
             acc[...] += jnp.dot(quotient, tile, preferred_element_type=F32)
@@ -242,7 +249,7 @@
         return to_tm(back_out.at[piece(i), :], back_in.at[piece(i), :], back_s.at[i],
                      back_r.at[i], lax.rem(now + slices - 1, slices))
 
-    lag = 3 * (slices - 1 - 2 * now)
+    lag = 2 * (slices - 1 - 2 * now)
     fwd_lag = jnp.maximum(-lag, 0)
     back_lag = jnp.maximum(lag, 0)
     both_lag = jnp.maximum(fwd_lag, back_lag)
@@ -286,7 +293,7 @@
             smooth_ref[at, :] = smoothed.astype(BF)
         return carry
 
-    lax.fori_loop(0, pieces + 3 * (slices - 1), step, 0)
+    lax.fori_loop(0, pieces + 2 * (slices - 1), step, 0)
     topics_ref[...] = settle(last)
 
     wait_bytes(stat_in.at[pl.ds(0, n - 1)], stat_s.at[0])
@@ -317,7 +324,7 @@
     words, topics = topic_means.shape[1:]
     every = docs * n
     word_tile = min(512, words // 2)
-    chunk = max(words // 32, 16)
+    chunk = max(words // 16, 16)
     pieces = words // chunk
     rounds = max(min(4, docs // 16), 1)
     dma = pltpu.SemaphoreType.DMA
@@ -331,6 +338,7 @@
         scratch_shapes=[
             pltpu.VMEM((n, docs, words), jnp.int32),
             pltpu.VMEM((n - 1, docs, words), BF),
+            pltpu.VMEM((every, words), BF),
             pltpu.VMEM((every, words), BF),
             pltpu.VMEM((words, topics), F32),
             pltpu.VMEM((words, topics), BF),

time: 144 us -> 138 us (0.958)
  Pallas kernels: 140 us -> 134 us
    pallas_call x1, Pallas kernels: 140 us -> 134 us  [body(): pl.pallas_call(functools.partial(round_kernel, n, slices, word_tile, chun...]
where the time goes in v7:
time: 138 us
  Pallas kernels  134 us (97%)
  other arithmetic  2.68 us (2%)
    pallas_call x1, Pallas kernels, body(): pl.pallas_call(functools.partial(round_kernel, n, slices, word_tile, chun...  134 us

profile of v7, /device:TPU:0, one launch (start us, length us, event | category | flops | bytes accessed | tf_op | source)
XLA Modules:
  0.0 138.3 jit_solution(17660336491522082799)
XLA Ops:
  0.6 134.3 %shard_map.77 = (bf16[4096,128]{1,0:T(8,128)(2,1)}, f32[64,128]{1,0:T(8,128)}) custom-call(s32[64,32768]{1,0:T(8,128)} %bitcast.10, f32[4096,128]{1,0:T(8,128)} %bitcast.11, f32[64,128]{1,0:T(8,128)} %bitcast.12, f32[1,128]{1,0:T(1,128)} %bitcast.14, f32[1,128]{1,0:T(1,128)} %bitcast.15, f32[1,128]{1,0:T(1,128)} %bitcast.16), custom_call_target="tpu_custom_call" | custom-call | tf_op jit(solution)/shard_map/pallas_call | solution.py:332
  135.0 0.0 copy-start
  135.0 2.7 %bitcast_convert_fusion = f32[1,4096,128]{2,1,0:T(8,128)} fusion(bf16[4096,128]{1,0:T(8,128)(2,1)} %get-tuple-element.4), kind=kLoop, calls=%fused_computation | loop fusion | flops 524288 | bytes 3145728 | tf_op jit(solution)/shard_map/broadcast_in_dim | solution.py:373
  137.7 0.0 copy-done
  137.7 0.6 copy.9
Async XLA Ops:
  135.0 2.7 %copy-start = (f32[64,128]{1,0:T(8,128)S(1)}, f32[64,128]{1,0:T(8,128)}, u32[]{:S(2)}) copy-start(f32[64,128]{1,0:T(8,128)} %get-tuple-element.5) | copy-start | bytes 98308
